TPU v7x, 256 devices: a whole 4x4x8 slice. The times are simulated.
256 devices in a mesh: eye: 2 (over core), row: 8 (over z_lo, x), col: 16 (over y, z_hi).
Axes of the slice: x: 4, y: 4, z: 8 (z_hi: 4, z_lo: 2; z = z_hi * 2 + z_lo), core: 2. Of those that a mesh axis runs over, the one named last changes fastest.
Arguments:
- images: bfloat16 [2, 160, 64, 2048], P('eye', 'row', None, 'col'), may hold values from -20 to 20, as said below
- cotangent: bfloat16 [2, 160, 64, 2048], P('eye', 'row', None, 'col'), may hold values from -6 to 6
- conv_weight: bfloat16 [3, 3, 64, 64], replicated, may hold values from -0.25 to 0.25
- query_weight: bfloat16 [64, 64], replicated, may hold values from -0.75 to 0.75
- key_weight: bfloat16 [64, 64], replicated, may hold values from -0.75 to 0.75
- band_start: int32 [2, 8, 16], P('eye', 'row', 'col'), may hold values from 0 to 1536, as said below
- band_width: int32 [2, 8, 16], P('eye', 'row', 'col'), may hold values from 128 to 512, as said below
Outputs:
- refined: bfloat16 [2, 160, 64, 2048], P('eye', 'row', None, 'col')
- input_grad: bfloat16 [2, 160, 64, 2048], P('eye', 'row', None, 'col')
- conv_grad: float32 [3, 3, 64, 64], replicated
- query_grad: float32 [64, 64], replicated
- key_grad: float32 [64, 64], replicated
Inputs may be any that keep to these rules, and one draw needn't show every extreme that they name: `images`: the shown draw lies within -4 to 4. `band_start`: A multiple of 128; start + 512 never passes the row's end. `band_width`: A multiple of 128.
All inputs are finite; a program needn't handle non-finite values.
Results may differ from a plain program's by a relative error of at most 0.014.
Values may be sent and summed in bfloat16 or wider, within the bound.
No kernel may reach another device: no remote copies, remote signals or barrier semaphores. Data moves between devices by JAX's collectives and lax.ppermute only.
A program may use at most 128 MiB of HBM per device.

v0:
```python
import jax
import jax.numpy as jnp
from jax import lax
from jax.sharding import PartitionSpec as P

BAND_PANELS = 4


def with_halo(block, sides, width):
    for axis, dim in sides:
        count = lax.axis_size(axis)
        forward = [(i, i + 1) for i in range(count - 1)]
        backward = [(target, source) for source, target in forward]
        low = lax.ppermute(
            lax.slice_in_dim(block, block.shape[dim] - width, None, axis=dim), axis, forward
        )
        high = lax.ppermute(lax.slice_in_dim(block, 0, width, axis=dim), axis, backward)
        block = jnp.concatenate([low, block, high], axis=dim)
    return block


def leaky(value):
    return jnp.where(value > 0, value, 0.1 * value)


def attend(query_block, grad_block, key_block, value_block, width, scale):
    scores = (
        jnp.einsum("hcp,hcj->hpj", query_block, key_block, preferred_element_type=jnp.float32)
        * scale
    )
    live = (jnp.arange(key_block.shape[2], dtype=jnp.int32) < width)[None, None, :]
    scores = jnp.where(live, scores, -jnp.inf)
    peak = jnp.max(scores, axis=2, keepdims=True)
    expo = jnp.where(live, jnp.exp(scores - peak), 0.0)
    prob = expo / jnp.sum(expo, axis=2, keepdims=True)
    prob_b = prob.astype(jnp.bfloat16)
    attended = jnp.einsum("hpj,hcj->hcp", prob_b, value_block, preferred_element_type=jnp.float32)
    dprob = jnp.einsum("hcp,hcj->hpj", grad_block, value_block, preferred_element_type=jnp.float32)
    delta = jnp.sum(prob * dprob, axis=2, keepdims=True)
    dscore = (scale * prob * (dprob - delta)).astype(jnp.bfloat16)
    dquery = jnp.einsum("hpj,hcj->hcp", dscore, key_block, preferred_element_type=jnp.float32)
    dkey = jnp.einsum("hpj,hcp->hcj", dscore, query_block, preferred_element_type=jnp.float32)
    dvalue = jnp.einsum("hpj,hcp->hcj", prob_b, grad_block, preferred_element_type=jnp.float32)
    return (attended, dquery, dkey, dvalue)


def body(images, cotangent, conv_weight, query_weight, key_weight, band_start, band_width):
    source = images[0]
    grad_out = cotangent[0]
    rows, chans, cols = source.shape
    scale = chans ** (-0.5)
    first = band_start[0, 0, 0]
    width = band_width[0, 0, 0]
    span = BAND_PANELS * cols
    full = cols * lax.axis_size("col")
    view = lax.axis_index("eye")
    padded = with_halo(source, (("row", 0), ("col", 2)), 1)
    conv = jnp.zeros((rows, chans, cols), jnp.float32)
    for a in range(3):
        for b in range(3):
            conv = conv + jnp.einsum(
                "io,hiw->how",
                conv_weight[a, b],
                padded[a : a + rows, :, b : b + cols],
                preferred_element_type=jnp.float32,
            )
    feat = (source.astype(jnp.float32) + leaky(conv)).astype(jnp.bfloat16)
    query = jnp.einsum(
        "io,hiw->how", query_weight, feat, preferred_element_type=jnp.float32
    ).astype(jnp.bfloat16)
    offset = (1 - view) * full + first

    def select_one(carry, piece):
        length = piece.shape[2]
        local = offset + jnp.arange(span, dtype=jnp.int32)
        valid = (local >= 0) & (local < length)
        widened = jnp.pad(piece, ((0, 0), (0, 0), (span, span)))
        where_from = jnp.clip(offset + span, 0, length + span)
        taken = lax.dynamic_slice_in_dim(widened, where_from, span, 2)
        return jnp.where(valid[None, None, :], taken, carry)

    empty = jnp.zeros((rows, chans, span), jnp.bfloat16)
    key_tile = jnp.einsum(
        "io,hiw->how", key_weight, feat, preferred_element_type=jnp.float32
    ).astype(jnp.bfloat16)
    carry = (empty, empty)
    key_band = select_one(carry[0], lax.all_gather(key_tile, ("eye", "col"), axis=2, tiled=True))
    value_band = select_one(carry[1], lax.all_gather(feat, ("eye", "col"), axis=2, tiled=True))
    block_rows = 4
    blocks = rows // block_rows

    def per_block(operands):
        query_block, grad_block, key_block, value_block = operands
        attended, dquery, dkey, dvalue = attend(
            query_block, grad_block, key_block, value_block, width, scale
        )
        dkey_b = dkey.astype(jnp.bfloat16)
        cross_part = (
            dvalue
            + jnp.einsum("io,hoj->hij", key_weight, dkey_b, preferred_element_type=jnp.float32)
        ).astype(jnp.bfloat16)
        key_part = jnp.einsum(
            "hij,hoj->io", value_block, dkey_b, preferred_element_type=jnp.float32
        )
        return (attended, dquery.astype(jnp.bfloat16), cross_part, key_part)

    attended, dquery_b, cross_part, key_parts = lax.map(
        per_block,
        (
            query.reshape(blocks, block_rows, chans, cols),
            grad_out.reshape(blocks, block_rows, chans, cols),
            key_band.reshape(blocks, block_rows, chans, span),
            value_band.reshape(blocks, block_rows, chans, span),
        ),
    )
    attended = attended.reshape(rows, chans, cols)
    dquery_b = dquery_b.reshape(rows, chans, cols)
    key_grad = jnp.sum(key_parts, axis=0)
    refined = (feat.astype(jnp.float32) + attended).astype(jnp.bfloat16)
    band_rows = jnp.transpose(cross_part.reshape(rows, chans, span), (2, 0, 1)).reshape(
        span, rows * chans
    )
    count = cols * lax.axis_size(("eye", "col"))
    shift_by = jnp.int32(0) - offset
    local = shift_by + jnp.arange(count, dtype=jnp.int32)
    valid = (local >= 0) & (local < span)
    widened = jnp.pad(band_rows, ((count, count), (0, 0)))
    where_from = jnp.clip(shift_by + count, 0, span + count)
    taken = lax.dynamic_slice_in_dim(widened, where_from, count, 0).astype(jnp.float32)
    arrived = lax.psum_scatter(
        jnp.where(valid[:, None], taken, 0.0).astype(jnp.bfloat16),
        ("eye", "col"),
        scatter_dimension=0,
        tiled=True,
    ).astype(jnp.float32)
    cross = jnp.transpose(arrived.reshape(cols, rows, chans), (1, 2, 0))
    dfeat = (
        grad_out.astype(jnp.float32)
        + jnp.einsum("io,how->hiw", query_weight, dquery_b, preferred_element_type=jnp.float32)
        + cross
    )
    dconv = (dfeat * jnp.where(conv > 0, 1.0, 0.1)).astype(jnp.bfloat16)
    dpad = with_halo(dconv, (("row", 0), ("col", 2)), 1)
    back = dfeat
    grads = []
    for a in range(3):
        line = []
        for b in range(3):
            back = back + jnp.einsum(
                "io,how->hiw",
                conv_weight[a, b],
                dpad[2 - a : 2 - a + rows, :, 2 - b : 2 - b + cols],
                preferred_element_type=jnp.float32,
            )
            line.append(
                jnp.einsum(
                    "hiw,how->io",
                    padded[a : a + rows, :, b : b + cols],
                    dconv,
                    preferred_element_type=jnp.float32,
                )
            )
        grads.append(jnp.stack(line))
    conv_local = jnp.stack(grads)
    query_local = jnp.einsum("hiw,how->io", feat, dquery_b, preferred_element_type=jnp.float32)
    conv_grad, query_grad, key_total = lax.psum(
        (conv_local, query_local, key_grad), ("eye", "row", "col")
    )
    return (refined[None], back.astype(jnp.bfloat16)[None], conv_grad, query_grad, key_total)


def solution(mesh):
    return jax.shard_map(
        body,
        mesh=mesh,
        in_specs=(
            P("eye", "row", None, "col"),
            P("eye", "row", None, "col"),
            P(),
            P(),
            P(),
            P("eye", "row", "col"),
            P("eye", "row", "col"),
        ),
        out_specs=(P("eye", "row", None, "col"), P("eye", "row", None, "col"), P(), P(), P()),
        check_vma=False,
    )
```

profile of v0, /device:TPU:1, one launch (start us, length us, event | category | flops | bytes accessed | tf_op | source)
XLA Modules:
  0.0 730.6 jit_solution(1525507267588658287)
XLA Ops:
  8.0 3.9 collective-permute-start
  14.6 1.9 collective-permute-done.1
  17.8 4.9 collective-permute-start.2
  24.6 3.8 collective-permute-done.2
  28.4 15.4 %collective-permute-done.3 = bf16[22,64,1]{2,1,0:T(8,128)(2,1)S(1)} collective-permute-done((bf16[22,64,1]{2,1,0:T(8,128)(2,1)S(1)}, bf16[22,64,1]{2,1,0:T(8,128)(2,1)S(1)}, u32[]{:S(2)}, u32[]{:S(2)}) %collective-permute-start.3) | collective-permute-done | bytes 2848 | tf_op jit(solution)/shard_map/ppermute | solution.py:17
  51.7 94.6 %all-gather.5.cloned.1.call-done = bf16[20,64,4096]{2,1,0:T(8,128)(2,1)} async-done(((bf16[20,64,128]{2,1,0:T(8,128)(2,1)}), bf16[20,64,4096]{2,1,0:T(8,128)(2,1)}) %all-gather.5.cloned.1.call-update) | async-done | bytes 10485776 | tf_op jit(solution)/shard_map/all_gather | solution.py:87
  146.4 98.4 %all-gather.3.cloned.1.call-done = bf16[20,64,4096]{2,1,0:T(8,128)(2,1)} async-done(((bf16[20,64,128]{2,1,0:T(8,128)(2,1)}), bf16[20,64,4096]{2,1,0:T(8,128)(2,1)}) %all-gather.3.cloned.1.call-update) | async-done | bytes 10485776 | tf_op jit(solution)/shard_map/all_gather | solution.py:88
  244.8 4.3 fusion.75
  249.1 61.7 %while.16 = (s32[]{:T(128)}, f32[5,4,64,128]{3,2,1,0:T(8,128)}, bf16[5,4,64,128]{3,2,1,0:T(8,128)(2,1)}, bf16[5,4,64,512]{3,2,1,0:T(8,128)(2,1)}, f32[5,64,64]{2...) while((s32[]{:T(128)}, f32[5,4,64,128]{3,2,1,0:T(8,128)}, ...), condition=%wide.region_4.5_spmd, body=%wide.region_0.4_spmd.sunk | while | flops 308972032 | bytes 11458313 | solution.py:107
  253.8 1.7 fusion.270
  257.3 1.9 fusion.269
  259.2 2.3 fusion.268
  266.2 1.7 fusion.270
  269.6 1.9 fusion.269
  271.5 2.3 fusion.268
  278.5 1.7 fusion.270
  282.0 1.9 fusion.269
  283.8 2.3 fusion.268
  294.3 1.9 fusion.269
  296.2 2.3 fusion.268
  303.2 1.7 fusion.270
  306.7 1.9 fusion.269
  308.5 2.3 fusion.268
  310.9 7.7 %select_convert_fusion = bf16[4096,1280]{0,1:T(8,128)(2,1)} fusion(s32[]{:T(128)S(6)} %min.9, bf16[512,1280]{0,1:T(8,128)(2,1)} %bitcast.395, pred[4096]{0:T(1024)(128)(4,1)} %fusion.168), kind=kLoop, calls=%fused_computation.60 | loop fusion | flops 15728640 | bytes 11800580 | tf_op jit(solution)/shard_map/convert_element_type | solution.py:131
  318.5 14.4 %copy.78 = bf16[4096,1280]{1,0:T(8,128)(2,1)} copy(bf16[4096,1280]{0,1:T(8,128)(2,1)} %select_convert_fusion) | data formatting | bytes 20971520
  334.3 77.4 %all-reduce.3 = (f32[64,64]{1,0:T(8,128)}, f32[64,64]{1,0:T(8,128)}) all-reduce(f32[64,64]{1,0:T(8,128)S(1)} %convolution_bitcast_fusion.15, f32[64,64]{1,0:T(8,128)S(1)} %reduce_sum.27), channel_id=1, replica_groups=mesh['eye'=2,'row'=8,'col'=16] {'eye','row','col'}, use_global_device_ids=true, to_apply=%region_7.8 | all-reduce | flops 8192 | bytes 65536 | tf_op jit(solution)/shard_map/psum | solution.py:166
  412.6 50.2 %reduce-scatter.4.cloned.1.call-done = bf16[128,1280]{1,0:T(8,128)(2,1)} async-done(((bf16[4096,1280]{1,0:T(8,128)(2,1)}), bf16[128,1280]{1,0:T(8,128)(2,1)}) %reduce-scatter.4.cloned.1.call-update) | async-done | bytes 327696
  468.3 4.2 collective-permute-start.4
  475.4 4.9 collective-permute-start.7
  480.8 3.9 collective-permute-done.6
  488.7 233.6 %all-reduce.6.cloned.1.call-done = f32[3,3,64,64]{3,2,1,0:T(8,128)} async-done(((f32[3,3,64,64]{3,2,1,0:T(8,128)}), f32[3,3,64,64]{3,2,1,0:T(8,128)}) %all-reduce.6.cloned.1.call-update) | async-done | bytes 147472 | tf_op jit(solution)/shard_map/psum | solution.py:166
  722.4 1.7 copy.111
  (193 shorter events, 62.1 us)
Async XLA Ops:
  7.2 43.3 %copy-start = (bf16[64,64]{1,0:T(8,128)(2,1)S(1)}, bf16[64,64]{1,0:T(8,128)(2,1)}, u32[]{:S(2)}) copy-start(bf16[64,64]{1,0:T(8,128)(2,1)} %param.12) | copy-start | bytes 24580
  7.2 139.2 %all-gather.5.cloned.1.call-start = ((), (), s32[]{:S(2)}) async-start(), calls=%async_computation.2 | async-start | bytes 10813440 | tf_op jit(solution)/shard_map/all_gather | solution.py:87
  8.0 6.7 collective-permute-start
  11.9 12.1 %copy-start.1 = (bf16[1,20,64,128]{3,2,1,0:T(8,128)(2,1)S(1)}, bf16[1,20,64,128]{3,2,1,0:T(8,128)(2,1)}, u32[]{:S(2)}) copy-start(bf16[1,20,64,128]{3,2,1,0:T(8,128)(2,1)} %param.9) | copy-start | bytes 983044
  11.9 12.1 %copy-start.11 = (bf16[3,3,64,64]{3,2,1,0:T(8,128)(2,1)S(1)}, bf16[3,3,64,64]{3,2,1,0:T(8,128)(2,1)}, u32[]{:S(2)}) copy-start(bf16[3,3,64,64]{3,2,1,0:T(8,128)(2,1)} %param.11) | copy-start | bytes 221188
  11.9 4.6 collective-permute-start.1
  14.6 29.1 %copy-start.17 = (bf16[1,64,128]{2,1,0:T(8,128)(2,1)}, bf16[1,64,128]{2,1,0:T(8,128)(2,1)S(1)}, u32[]{:S(2)}) copy-start(bf16[1,64,128]{2,1,0:T(8,128)(2,1)S(1)} %collective-permute-done) | copy-start | bytes 49156
  16.5 27.2 %copy-start.19 = (bf16[1,64,128]{2,1,0:T(8,128)(2,1)}, bf16[1,64,128]{2,1,0:T(8,128)(2,1)S(1)}, u32[]{:S(2)}) copy-start(bf16[1,64,128]{2,1,0:T(8,128)(2,1)S(1)} %collective-permute-done.1) | copy-start | bytes 49156
  17.8 10.6 %collective-permute-start.2 = (bf16[22,64,1]{2,1,0:T(8,128)(2,1)S(1)}, bf16[22,64,1]{2,1,0:T(8,128)(2,1)S(1)}, u32[]{:S(2)}, u32[]{:S(2)}) collective-permute-start(bf16[22,64,1]{2,1,0:T(8,128)(2,1)S(1)} %get-tuple-element.103), channel_id=1, source_target_pairs={{0,1},{1,2},{2,3},{3,4},{4,5},{5,6},{6,7},{7,8},{8,9},{9,10},{10,1... | collective-permute-start | bytes 8456 | tf_op jit(solution)/shard_map/ppermute | solution.py:14
  22.7 21.1 %collective-permute-start.3 = (bf16[22,64,1]{2,1,0:T(8,128)(2,1)S(1)}, bf16[22,64,1]{2,1,0:T(8,128)(2,1)S(1)}, u32[]{:S(2)}, u32[]{:S(2)}) collective-permute-start(bf16[22,64,1]{2,1,0:T(8,128)(2,1)S(1)} %get-tuple-element.104), channel_id=1, source_target_pairs={{1,0},{2,1},{3,2},{4,3},{5,4},{6,5},{7,6},{8,7},{9,8},{10,9},{11,1... | collective-permute-start | bytes 8456 | tf_op jit(solution)/shard_map/ppermute | solution.py:17
  48.3 196.4 %all-gather.3.cloned.1.call-start = ((), (), s32[]{:S(2)}) async-start(), calls=%async_computation.1 | async-start | bytes 10813440 | tf_op jit(solution)/shard_map/all_gather | solution.py:88
  49.1 413.7 %reduce-scatter.4.cloned.1.call-start = ((), (), s32[]{:S(2)}) async-start(), calls=%async_computation.4 | async-start | bytes 10813440
  255.5 3.7 copy-start.22
  255.5 3.7 copy-start.24
  267.8 3.7 copy-start.22
  267.8 3.7 copy-start.24
  280.2 3.6 copy-start.22
  292.5 3.7 copy-start.22
  292.5 3.7 copy-start.24
  304.9 3.7 copy-start.22
  304.9 3.7 copy-start.24
  332.9 78.8 %copy-start.10 = (f32[5,4,64,128]{3,2,1,0:T(8,128)S(1)}, f32[5,4,64,128]{3,2,1,0:T(8,128)}, u32[]{:S(2)}) copy-start(f32[5,4,64,128]{3,2,1,0:T(8,128)} %get-tuple-element.65) | copy-start | bytes 1966084
  333.0 389.4 %all-reduce.6.cloned.1.call-start = ((), (), s32[]{:S(2)}) async-start(), calls=%async_computation.3 | async-start | bytes 589824 | tf_op jit(solution)/shard_map/psum | solution.py:166
  333.8 130.1 %copy-start.8 = (f32[20,64,128]{2,1,0:T(8,128)S(1)}, f32[20,64,128]{2,1,0:T(8,128)}, u32[]{:S(2)}) copy-start(f32[20,64,128]{2,1,0:T(8,128)} %get-tuple-element.112) | copy-start | bytes 1966084
  333.8 130.1 %copy-start.15 = (bf16[5,4,64,128]{3,2,1,0:T(8,128)(2,1)S(1)}, bf16[5,4,64,128]{3,2,1,0:T(8,128)(2,1)}, u32[]{:S(2)}) copy-start(bf16[5,4,64,128]{3,2,1,0:T(8,128)(2,1)} %get-tuple-element.255) | copy-start | bytes 983044
  465.9 6.5 copy-start.20
  466.2 6.6 copy-start.18
  467.0 6.8 collective-permute-start.5
  468.3 5.5 collective-permute-start.4
  473.0 7.3 copy-start.12
  474.1 10.6 %collective-permute-start.6 = (bf16[22,64,1]{2,1,0:T(8,128)(2,1)S(1)}, bf16[22,64,1]{2,1,0:T(8,128)(2,1)S(1)}, u32[]{:S(2)}, u32[]{:S(2)}) collective-permute-start(bf16[22,64,1]{2,1,0:T(8,128)(2,1)S(1)} %get-tuple-element.99), channel_id=1, source_target_pairs={{1,0},{2,1},{3,2},{4,3},{5,4},{6,5},{7,6},{8,7},{9,8},{10,9},{11,1... | collective-permute-start | bytes 8456 | tf_op jit(solution)/shard_map/ppermute | solution.py:17
  475.4 10.2 %collective-permute-start.7 = (bf16[22,64,1]{2,1,0:T(8,128)(2,1)S(1)}, bf16[22,64,1]{2,1,0:T(8,128)(2,1)S(1)}, u32[]{:S(2)}, u32[]{:S(2)}) collective-permute-start(bf16[22,64,1]{2,1,0:T(8,128)(2,1)S(1)} %get-tuple-element.100), channel_id=1, source_target_pairs={{0,1},{1,2},{2,3},{3,4},{4,5},{5,6},{6,7},{7,8},{8,9},{9,10},{10,1... | collective-permute-start | bytes 8456 | tf_op jit(solution)/shard_map/ppermute | solution.py:14
  (25 other events, 43.8 us)
Sparse Core Ops, SparseCore 0:
  48.5 97.8 all-gather.4
  148.8 95.8 all-gather.2
  333.1 129.6 reduce-scatter.3
  473.9 248.4 all-reduce.5
where the time goes:
time: 733 us; the launch traced here: 731 us
  waiting for transfers between devices  504 us (69%)
  blocking collectives  77.4 us (11%)
  matrix products  66.2 us (9%)
  other arithmetic  24.2 us (3%)
  starting transfers between devices  23.4 us (3%)
  local copies, waits for them, and re-layouts  20.5 us (3%)
  between operations  15 us (2%)
    psum x1, waiting for transfers between devices, body(): lax.psum((conv_local, query_local, key_grad), ('eye', 'row', 'col'))  234 us
    all_gather x1, waiting for transfers between devices, body(): lax.all_gather(feat, ('eye', 'col'), axis=2, tiled=True)  98.4 us
    all_gather x1, waiting for transfers between devices, body(): lax.all_gather(key_tile, ('eye', 'col'), axis=2, tiled=True)  94.6 us
    psum x1, blocking collectives, body(): lax.psum((conv_local, query_local, key_grad), ('eye', 'row', 'col'))  77.4 us
    unnamed x5, waiting for transfers between devices  50.9 us
    ppermute x4, waiting for transfers between devices, with_halo(): lax.ppermute(lax.slice_in_dim(block, 0, width, axis=dim), axis, backward)  21.2 us
    unnamed x43, local copies, waits for them, and re-layouts  19.2 us
    ppermute x4, starting transfers between devices, with_halo(): lax.ppermute(lax.slice_in_dim(block, block.shape[dim] - width, None, axis...  17.9 us
  transfers between devices with their start and end apart: 12, of which 9 were waited for; matrix products, arithmetic and copies ran while one was open for 1% of the time, Pallas kernels for 0%

commit v1 on v0

v1 whole, which is shorter than its diff:
```python
import functools

import jax
import jax.numpy as jnp
from jax import lax
from jax.experimental import pallas as pl
from jax.experimental.pallas import tpu as pltpu
from jax.sharding import PartitionSpec as P

BAND_PANELS = 4


def with_halo(block, sides, width):
    for axis, dim in sides:
        count = lax.axis_size(axis)
        forward = [(i, i + 1) for i in range(count - 1)]
        backward = [(target, source) for source, target in forward]
        low = lax.ppermute(
            lax.slice_in_dim(block, block.shape[dim] - width, None, axis=dim), axis, forward
        )
        high = lax.ppermute(lax.slice_in_dim(block, 0, width, axis=dim), axis, backward)
        block = jnp.concatenate([low, block, high], axis=dim)
    return block


def leaky(value):
    return jnp.where(value > 0, value, 0.1 * value)


def dot(lhs, rhs, dims):
    return lax.dot_general(lhs, rhs, (dims, ((), ())), preferred_element_type=jnp.float32)


NN = ((1,), (0,))
NT = ((1,), (1,))
TN = ((0,), (0,))


def attend_kernel(
    scale, live_ref, wq_ref, wk_ref, feat_ref, grad_ref, v0_ref, v1_ref, v2_ref, v3_ref,
    refined_ref, part_ref, x0_ref, x1_ref, x2_ref, x3_ref, qsum_ref, ksum_ref,
):
    values = (v0_ref, v1_ref, v2_ref, v3_ref)
    crosses = (x0_ref, x1_ref, x2_ref, x3_ref)
    cols = feat_ref.shape[2]
    wq = wq_ref[...]
    wk = wk_ref[...]
    wq_t = wq.T
    wk_t = wk.T

    @pl.when(pl.program_id(0) == 0)
    def _():
        qsum_ref[...] = jnp.zeros_like(qsum_ref)
        ksum_ref[...] = jnp.zeros_like(ksum_ref)

    qsum = jnp.zeros(qsum_ref.shape, jnp.float32)
    ksum = jnp.zeros(ksum_ref.shape, jnp.float32)
    for h in range(feat_ref.shape[0]):
        feat = feat_ref[h]
        grad = grad_ref[h]
        value = jnp.concatenate([ref[h] for ref in values], axis=1)
        key = dot(wk_t, value, NN).astype(jnp.bfloat16)
        query = dot(wq_t, feat, NN).astype(jnp.bfloat16)
        query_t = dot(feat.T, wq, NN).astype(jnp.bfloat16)
        score = dot(query_t, key, NN) * scale
        score = jnp.concatenate(
            [
                jnp.where(live_ref[o] > 0, score[:, o * cols : (o + 1) * cols], -jnp.inf)
                for o in range(BAND_PANELS)
            ],
            axis=1,
        )
        peak = jnp.max(score, axis=1, keepdims=True)
        expo = jnp.exp(score - peak)
        prob = expo * (1.0 / jnp.sum(expo, axis=1, keepdims=True))
        prob_b = prob.astype(jnp.bfloat16)
        dprob = dot(grad.T, value, NN)
        delta = jnp.sum(prob * dprob, axis=1, keepdims=True)
        dscore = (scale * prob * (dprob - delta)).astype(jnp.bfloat16)
        attended = dot(value, prob_b, NT)
        refined_ref[h] = (feat.astype(jnp.float32) + attended).astype(jnp.bfloat16)
        dquery = dot(key, dscore, NT).astype(jnp.bfloat16)
        dkey = dot(query, dscore, NN).astype(jnp.bfloat16)
        cross = (dot(grad, prob_b, NN) + dot(wk, dkey, NN)).astype(jnp.bfloat16)
        for o in range(BAND_PANELS):
            crosses[o][h] = cross[:, o * cols : (o + 1) * cols]
        part_ref[h] = grad.astype(jnp.float32) + dot(wq, dquery, NN)
        qsum = qsum + dot(feat, dquery, NT)
        ksum = ksum + dot(value, dkey, NT)
    qsum_ref[...] += qsum
    ksum_ref[...] += ksum


def attend(live, wq, wk, feat, grad, values, block_rows=4):
    rows, chans, cols = feat.shape
    tile = pl.BlockSpec((block_rows, chans, cols), lambda i: (i, 0, 0))
    square = pl.BlockSpec((chans, chans), lambda i: (0, 0))
    tile_b = jax.ShapeDtypeStruct((rows, chans, cols), jnp.bfloat16)
    tile_f = jax.ShapeDtypeStruct((rows, chans, cols), jnp.float32)
    square_f = jax.ShapeDtypeStruct((chans, chans), jnp.float32)
    flops = 2 * rows * chans * cols * cols * BAND_PANELS * 7
    return pl.pallas_call(
        functools.partial(attend_kernel, chans ** -0.5),
        grid=(rows // block_rows,),
        in_specs=[pl.BlockSpec(memory_space=pltpu.SMEM), square, square] + [tile] * 6,
        out_specs=[tile] * 6 + [square, square],
        out_shape=[tile_b, tile_f] + [tile_b] * 4 + [square_f, square_f],
        compiler_params=pltpu.CompilerParams(vmem_limit_bytes=48 * 1024 * 1024),
        cost_estimate=pl.CostEstimate(
            flops=flops, bytes_accessed=13 * rows * chans * cols * 2, transcendentals=rows * cols * cols * 4
        ),
    )(live, wq, wk, feat, grad, *values)


def along_y(block, shift, ny, nz):
    perm = [(y * nz + z, ((y + shift) % ny) * nz + z) for y in range(ny) for z in range(nz)]
    return lax.ppermute(block, "col", perm)


def across(block, shift, ny, nz):
    perm = [
        (e * ny * nz + y * nz + z, (1 - e) * ny * nz + y * nz + (z + shift) % nz)
        for e in range(2)
        for y in range(ny)
        for z in range(nz)
    ]
    return lax.ppermute(block, ("eye", "col"), perm)


def sum_all(total):
    total = total + lax.ppermute(total, "eye", [(0, 1), (1, 0)])
    n_row = lax.axis_size("row")
    n_col = lax.axis_size("col")
    lines, lanes = total.shape
    pieces = lax.all_to_all(total.reshape(n_row, lines // n_row, lanes), "row", 0, 0)
    piece = jnp.sum(pieces, axis=0)
    spread = lax.all_to_all(jnp.broadcast_to(piece[None], (n_col,) + piece.shape), "col", 0, 0)
    piece = jnp.sum(spread, axis=0)
    back = lax.all_to_all(jnp.broadcast_to(piece[None], (n_row,) + piece.shape), "row", 0, 0)
    return back.reshape(lines, lanes)


def body(images, cotangent, conv_weight, query_weight, key_weight, band_start, band_width):
    source = images[0]
    grad_out = cotangent[0]
    rows, chans, cols = source.shape
    nz = BAND_PANELS
    ny = lax.axis_size("col") // nz
    col = lax.axis_index("col")
    eye = lax.axis_index("eye")
    my_y = col // nz
    my_z = col % nz
    panel = band_start[0, 0, 0] // cols
    width = band_width[0, 0, 0]
    starts = lax.all_gather(band_start.reshape(1) // cols, ("eye", "col"), axis=0, tiled=True)

    padded = with_halo(source, (("row", 0), ("col", 2)), 1)
    conv = jnp.zeros((rows, chans, cols), jnp.float32)
    for a in range(3):
        for b in range(3):
            conv = conv + jnp.einsum(
                "io,hiw->how",
                conv_weight[a, b],
                padded[a : a + rows, :, b : b + cols],
                preferred_element_type=jnp.float32,
            )
    feat = (source.astype(jnp.float32) + leaky(conv)).astype(jnp.bfloat16)

    held = [feat] + [along_y(feat, shift, ny, nz) for shift in range(1, ny)]
    picks = []
    values = []
    for shift in range(nz):
        target = lax.dynamic_index_in_dim(
            starts, (1 - eye) * ny * nz + my_y * nz + (my_z + shift) % nz, 0, False
        )
        wanted = target + (my_z - target) % nz
        pick = (my_y - wanted // nz) % ny
        picks.append(pick)
        chosen = held[0]
        for k in range(1, ny):
            chosen = jnp.where(pick == k, held[k], chosen)
        values.append(across(chosen, shift, ny, nz))
    place = (my_z - jnp.arange(nz, dtype=jnp.int32) - panel) % nz
    live = (place * cols < width).astype(jnp.int32)

    refined, part, *crosses, query_local, key_local = attend(
        live, query_weight, key_weight, feat, grad_out, values
    )

    returned = [
        across(crosses[shift], -shift, ny, nz).astype(jnp.float32) for shift in range(nz)
    ]
    cross = part
    for k in range(ny):
        total = jnp.zeros((rows, chans, cols), jnp.float32)
        for shift in range(nz):
            total = total + jnp.where(picks[shift] == k, returned[shift], 0.0)
        if k > 0:
            total = along_y(total.astype(jnp.bfloat16), -k, ny, nz).astype(jnp.float32)
        cross = cross + total
    dfeat = cross
    dconv = (dfeat * jnp.where(conv > 0, 1.0, 0.1)).astype(jnp.bfloat16)
    dpad = with_halo(dconv, (("row", 0), ("col", 2)), 1)
    back = dfeat
    grads = []
    for a in range(3):
        for b in range(3):
            back = back + jnp.einsum(
                "io,how->hiw",
                conv_weight[a, b],
                dpad[2 - a : 2 - a + rows, :, 2 - b : 2 - b + cols],
                preferred_element_type=jnp.float32,
            )
            grads.append(
                jnp.einsum(
                    "hiw,how->io",
                    padded[a : a + rows, :, b : b + cols],
                    dconv,
                    preferred_element_type=jnp.float32,
                )
            )
    total = sum_all(jnp.concatenate(grads + [query_local, key_local], axis=0))
    total = total.reshape(11, chans, chans)
    conv_grad = total[:9].reshape(3, 3, chans, chans)
    return (refined[None], back.astype(jnp.bfloat16)[None], conv_grad, total[9], total[10])


def solution(mesh):
    return jax.shard_map(
        body,
        mesh=mesh,
        in_specs=(
            P("eye", "row", None, "col"),
            P("eye", "row", None, "col"),
            P(),
            P(),
            P(),
            P("eye", "row", "col"),
            P("eye", "row", "col"),
        ),
        out_specs=(P("eye", "row", None, "col"), P("eye", "row", None, "col"), P(), P(), P()),
        check_vma=False,
    )
```

time: 733 us -> 270 us (0.37)
  waiting for transfers between devices: 504 us -> 115 us
  blocking collectives: 77.4 us -> 20.3 us
  matrix products: 66.2 us -> 13.2 us
  starting transfers between devices: 23.4 us -> 73.7 us
  Pallas kernels: 0 us -> 18 us
  other arithmetic: 24.2 us -> 8.68 us
  local copies, waits for them, and re-layouts: 20.5 us -> 7.39 us
    psum x1 -> x0, waiting for transfers between devices: 234 us -> none  [body(): lax.psum((conv_local, query_local, key_grad), ('eye', 'row', 'col'))]
    all_gather x2 -> x0, waiting for transfers between devices: 193 us -> none  [the longest x1 98.4 us: body(): lax.all_gather(feat, ('eye', 'col'), axis=2, tiled=True)]
    psum x1 -> x0, blocking collectives: 77.4 us -> none  [body(): lax.psum((conv_local, query_local, key_grad), ('eye', 'row', 'col'))]
    ppermute x0 -> x15, waiting for transfers between devices: none -> 68.7 us  [the longest x8 51.4 us: across(): return lax.ppermute(block, ('eye', 'col'), perm)]
    unnamed x5 -> x0, waiting for transfers between devices: 50.9 us -> none
    dot_general x39 -> x0, matrix products: 48.4 us -> none  [the longest x5 11.6 us: attend(): jnp.einsum('hpj,hcj->hcp', prob_b, value_block, preferred_element_type=jn...]
    all_to_all x0 -> x3, starting transfers between devices: none -> 29.1 us  [the longest x1 17.4 us: sum_all(): lax.all_to_all(total.reshape(n_row, lines // n_row, lanes), 'row', 0, 0)]
    ppermute x0 -> x15, starting transfers between devices: none -> 20.4 us  [the longest x8 13.8 us: across(): return lax.ppermute(block, ('eye', 'col'), perm)]
  transfers between devices with their start and end apart: 12 -> 26, of which waited for: 9 -> 14; matrix products, arithmetic and copies ran while one was open for 1% -> 5% of each run, Pallas kernels for 0% -> 0%
where the time goes in v1:
time: 270 us; the launch traced here: 265 us
  waiting for transfers between devices  115 us (43%)
  starting transfers between devices  73.7 us (27%)
  blocking collectives  20.3 us (8%)
  Pallas kernels  18 us (7%)
  matrix products  13.2 us (5%)
  other arithmetic  8.68 us (3%)
  between operations  7.89 us (3%)
  local copies, waits for them, and re-layouts  7.39 us (3%)
    ppermute x8, waiting for transfers between devices, across(): return lax.ppermute(block, ('eye', 'col'), perm)  51.4 us
    ppermute x4, waiting for transfers between devices, with_halo(): lax.ppermute(lax.slice_in_dim(block, 0, width, axis=dim), axis, backward)  22 us
    unnamed x1, blocking collectives  20.3 us
    ppermute x4, starting transfers between devices, with_halo(): lax.ppermute(lax.slice_in_dim(block, block.shape[dim] - width, None, axis...  19.1 us
    pallas_call x1, Pallas kernels, attend(): pl.pallas_call(functools.partial(attend_kernel, chans ** (-0.5)), grid=(r...  18 us
    all_to_all x1, starting transfers between devices, sum_all(): lax.all_to_all(total.reshape(n_row, lines // n_row, lanes), 'row', 0, 0)  17.4 us
    ppermute x6, waiting for transfers between devices, along_y(): return lax.ppermute(block, 'col', perm)  17.3 us
    ppermute x8, starting transfers between devices, across(): return lax.ppermute(block, ('eye', 'col'), perm)  13.8 us
  transfers between devices with their start and end apart: 26, of which 14 were waited for; matrix products, arithmetic and copies ran while one was open for 5% of the time, Pallas kernels for 0%

profile of v1, /device:TPU:1, one launch (start us, length us, event | category | flops | bytes accessed | tf_op | source)
XLA Modules:
  0.0 264.5 jit_solution(11778186410655130124)
XLA Ops:
  1.4 3.9 %collective-permute-start = (bf16[1,64,128]{2,1,0:T(8,128)(2,1)S(1)}, bf16[1,64,128]{2,1,0:T(8,128)(2,1)S(1)}, u32[]{:S(2)}, u32[]{:S(2)}) collective-permute-start(bf16[1,64,128]{2,1,0:T(8,128)(2,1)S(1)} %get-tuple-element.42), channel_id=1, source_target_pairs={{0,16},{16,32},{32,48},{48,64},{64,80},{80,96},{96,112},{1,17},{17... | collective-permute-start | bytes 49160 | tf_op jit(solution)/shard_map/ppermute | solution.py:18
  7.9 1.9 collective-permute-done.1
  10.1 4.9 %collective-permute-start.2 = (bf16[22,64,1]{2,1,0:T(8,128)(2,1)S(1)}, bf16[22,64,1]{2,1,0:T(8,128)(2,1)S(1)}, u32[]{:S(2)}, u32[]{:S(2)}) collective-permute-start(bf16[22,64,1]{2,1,0:T(8,128)(2,1)S(1)} %get-tuple-element.38), channel_id=1, source_target_pairs={{0,1},{1,2},{2,3},{3,4},{4,5},{5,6},{6,7},{7,8},{8,9},{9,10},{10,1... | collective-permute-start | bytes 8456 | tf_op jit(solution)/shard_map/ppermute | solution.py:18
  16.9 3.9 %collective-permute-done.2 = bf16[22,64,1]{2,1,0:T(8,128)(2,1)S(1)} collective-permute-done((bf16[22,64,1]{2,1,0:T(8,128)(2,1)S(1)}, bf16[22,64,1]{2,1,0:T(8,128)(2,1)S(1)}, u32[]{:S(2)}, u32[]{:S(2)}) %collective-permute-start.2) | collective-permute-done | bytes 2848 | tf_op jit(solution)/shard_map/ppermute | solution.py:18
  20.7 15.4 %collective-permute-done.3 = bf16[22,64,1]{2,1,0:T(8,128)(2,1)S(1)} collective-permute-done((bf16[22,64,1]{2,1,0:T(8,128)(2,1)S(1)}, bf16[22,64,1]{2,1,0:T(8,128)(2,1)S(1)}, u32[]{:S(2)}, u32[]{:S(2)}) %collective-permute-start.3) | collective-permute-done | bytes 2848 | tf_op jit(solution)/shard_map/ppermute | solution.py:21
  38.2 1.3 fusion.30
  39.5 2.7 %collective-permute-start.4 = (bf16[20,64,128]{2,1,0:T(8,128)(2,1)S(1)}, bf16[20,64,128]{2,1,0:T(8,128)(2,1)S(1)}, u32[]{:S(2)}, u32[]{:S(2)}) collective-permute-start(bf16[20,64,128]{2,1,0:T(8,128)(2,1)S(1)} %get-tuple-element.48.feat_ref), channel_id=1, source_target_pairs={{0,12},{1,13},{2,14},{3,15},{4,0},{5,1},{6,2},{7,3},{8,4},{9,5},{1... | collective-permute-start | bytes 983048 | tf_op jit(solution)/shard_map/ppermute | solution.py:117
  44.2 20.3 %all-reduce = s32[32]{0:T(128)S(1)} all-reduce(s32[32]{0:T(128)S(1)} %fusion.131), channel_id=1, replica_groups=mesh['eye'=2,'row'=8,'col'=16] {'eye','col'}, use_global_device_ids=true, to_apply=%add | all-reduce | flops 32 | bytes 256
  71.5 4.3 %collective-permute-start.10 = (bf16[20,64,128]{2,1,0:T(8,128)(2,1)}, bf16[20,64,128]{2,1,0:T(8,128)(2,1)S(1)}, u32[]{:S(2)}, u32[]{:S(2)}) collective-permute-start(bf16[20,64,128]{2,1,0:T(8,128)(2,1)} %get-tuple-element.26), channel_id=1, source_target_pairs={{0,131},{1,128},{2,129},{3,130},{4,135},{5,132},{6,133},{7,134},{8... | collective-permute-start | bytes 983048 | tf_op jit(solution)/shard_map/ppermute | solution.py:127
  75.8 1.4 collective-permute-start.9
  79.0 25.6 %collective-permute-done.10.v3_ref = bf16[20,64,128]{2,1,0:T(8,128)(2,1)S(1)} collective-permute-done((bf16[20,64,128]{2,1,0:T(8,128)(2,1)}, bf16[20,64,128]{2,1,0:T(8,128)(2,1)S(1)}, u32[]{:S(2)}, u32[]{:S(2)}) %collective-permute-start.10) | collective-permute-done | bytes 327712 | tf_op jit(solution)/shard_map/ppermute | solution.py:127
  104.6 18.0 %shard_map.110 = (bf16[20,64,128]{2,1,0:T(8,128)(2,1)}, f32[20,64,128]{2,1,0:T(8,128)S(1)}, bf16[20,64,128]{2,1,0:T(8,128)(2,1)S(1)}, bf16[20,64,128]{2,1,0:T(8,...) custom-call(s32[4]{0:T(128)S(1)} %compare_convert_fusion.live_ref, ...), custom_call_target="tpu_custom_call" | custom-call | flops 1174405120 | bytes 4259840 | tf_op jit(solution)/shard_map/pallas_call | solution.py:102
  123.2 4.0 %collective-permute-start.12 = (bf16[20,64,128]{2,1,0:T(8,128)(2,1)S(1)}, bf16[20,64,128]{2,1,0:T(8,128)(2,1)S(1)}, u32[]{:S(2)}, u32[]{:S(2)}) collective-permute-start(bf16[20,64,128]{2,1,0:T(8,128)(2,1)S(1)} %get-tuple-element.16), channel_id=1, source_target_pairs={{0,131},{1,128},{2,129},{3,130},{4,135},{5,132},{6,133},{7,134},{8... | collective-permute-start | bytes 983048 | tf_op jit(solution)/shard_map/ppermute | solution.py:127
  127.2 2.3 collective-permute-start.14
  129.6 25.8 %collective-permute-done.12 = bf16[20,64,128]{2,1,0:T(8,128)(2,1)S(1)} collective-permute-done((bf16[20,64,128]{2,1,0:T(8,128)(2,1)S(1)}, bf16[20,64,128]{2,1,0:T(8,128)(2,1)S(1)}, u32[]{:S(2)}, u32[]{:S(2)}) %collective-permute-start.12) | collective-permute-done | bytes 327712 | tf_op jit(solution)/shard_map/ppermute | solution.py:127
  155.4 1.5 fusion.41
  156.9 2.7 %collective-permute-start.15 = (bf16[20,64,128]{2,1,0:T(8,128)(2,1)}, bf16[20,64,128]{2,1,0:T(8,128)(2,1)S(1)}, u32[]{:S(2)}, u32[]{:S(2)}) collective-permute-start(bf16[20,64,128]{2,1,0:T(8,128)(2,1)} %get-tuple-element.23), channel_id=1, source_target_pairs={{0,12},{1,13},{2,14},{3,15},{4,0},{5,1},{6,2},{7,3},{8,4},{9,5},{1... | collective-permute-start | bytes 983048 | tf_op jit(solution)/shard_map/ppermute | solution.py:117
  160.1 6.7 %collective-permute-done.15 = bf16[20,64,128]{2,1,0:T(8,128)(2,1)S(1)} collective-permute-done((bf16[20,64,128]{2,1,0:T(8,128)(2,1)}, bf16[20,64,128]{2,1,0:T(8,128)(2,1)S(1)}, u32[]{:S(2)}, u32[]{:S(2)}) %collective-permute-start.15) | collective-permute-done | bytes 327712 | tf_op jit(solution)/shard_map/ppermute | solution.py:117
  166.8 2.6 collective-permute-done.16
  169.4 7.9 %collective-permute-done.17 = bf16[20,64,128]{2,1,0:T(8,128)(2,1)} collective-permute-done((bf16[20,64,128]{2,1,0:T(8,128)(2,1)}, bf16[20,64,128]{2,1,0:T(8,128)(2,1)}, u32[]{:S(2)}, u32[]{:S(2)}) %collective-permute-start.17) | collective-permute-done | bytes 327712 | tf_op jit(solution)/shard_map/ppermute | solution.py:117
  177.3 2.6 fusion.28
  180.2 3.8 %collective-permute-start.18 = (bf16[1,64,128]{2,1,0:T(8,128)(2,1)S(1)}, bf16[1,64,128]{2,1,0:T(8,128)(2,1)S(1)}, u32[]{:S(2)}, u32[]{:S(2)}) collective-permute-start(bf16[1,64,128]{2,1,0:T(8,128)(2,1)S(1)} %get-tuple-element.40), channel_id=1, source_target_pairs={{0,16},{16,32},{32,48},{48,64},{64,80},{80,96},{96,112},{1,17},{17... | collective-permute-start | bytes 49160 | tf_op jit(solution)/shard_map/ppermute | solution.py:18
  190.1 6.4 %collective-permute-start.21 = (bf16[22,64,1]{2,1,0:T(8,128)(2,1)S(1)}, bf16[22,64,1]{2,1,0:T(8,128)(2,1)S(1)}, u32[]{:S(2)}, u32[]{:S(2)}) collective-permute-start(bf16[22,64,1]{2,1,0:T(8,128)(2,1)S(1)} %get-tuple-element.35), channel_id=1, source_target_pairs={{0,1},{1,2},{2,3},{3,4},{4,5},{5,6},{6,7},{7,8},{8,9},{9,10},{10,1... | collective-permute-start | bytes 8456 | tf_op jit(solution)/shard_map/ppermute | solution.py:18
  197.0 4.5 %collective-permute-done.20 = bf16[22,64,1]{2,1,0:T(8,128)(2,1)S(1)} collective-permute-done((bf16[22,64,1]{2,1,0:T(8,128)(2,1)S(1)}, bf16[22,64,1]{2,1,0:T(8,128)(2,1)S(1)}, u32[]{:S(2)}, u32[]{:S(2)}) %collective-permute-start.20) | collective-permute-done | bytes 2848 | tf_op jit(solution)/shard_map/ppermute | solution.py:21
  203.6 1.8 copy.94
  205.4 17.4 %all-to-all-start = ((f32[8,88,64]{1,2,0:T(8,128)}), f32[8,88,64]{1,2,0:T(8,128)S(1)}, u32[]{:S(2)}, u32[]{:S(2)}) async-start(f32[8,88,64]{1,2,0:T(8,128)} %copy.94), calls=%async_computation | async-start | bytes 524288 | tf_op jit(solution)/shard_map/all_to_all | solution.py:135
  225.1 3.9 %all-to-all-done = f32[8,88,64]{1,2,0:T(8,128)S(1)} async-done(((f32[8,88,64]{1,2,0:T(8,128)}), f32[8,88,64]{1,2,0:T(8,128)S(1)}, u32[]{:S(2)}, u32[]{:S(2)}) %all-to-all-start) | async-done | bytes 180256 | tf_op jit(solution)/shard_map/all_to_all | solution.py:135
  229.8 8.3 %all-to-all-start.1 = ((f32[16,88,64]{1,2,0:T(8,128)}), f32[16,88,64]{1,2,0:T(8,128)}, u32[]{:S(2)}, u32[]{:S(2)}) async-start(f32[16,88,64]{1,2,0:T(8,128)} %broadcast_in_dim.44), calls=%async_computation.1 | async-start | bytes 1048576 | tf_op jit(solution)/shard_map/all_to_all | solution.py:137
  238.1 1.8 fusion.8
  240.4 11.3 %all-to-all-done.1 = f32[16,88,64]{1,2,0:T(8,128)} async-done(((f32[16,88,64]{1,2,0:T(8,128)}), f32[16,88,64]{1,2,0:T(8,128)}, u32[]{:S(2)}, u32[]{:S(2)}) %all-to-all-start.1) | async-done | bytes 360480 | tf_op jit(solution)/shard_map/all_to_all | solution.py:137
  253.6 3.4 %all-to-all-start.2 = ((f32[8,88,64]{1,2,0:T(8,128)}), f32[8,88,64]{1,2,0:T(8,128)S(1)}, u32[]{:S(2)}, u32[]{:S(2)}) async-start(f32[8,88,64]{1,2,0:T(8,128)} %broadcast_in_dim.45), calls=%async_computation.2 | async-start | bytes 524288 | tf_op jit(solution)/shard_map/all_to_all | solution.py:139
  258.3 4.7 %all-to-all-done.2 = f32[8,88,64]{1,2,0:T(8,128)S(1)} async-done(((f32[8,88,64]{1,2,0:T(8,128)}), f32[8,88,64]{1,2,0:T(8,128)S(1)}, u32[]{:S(2)}, u32[]{:S(2)}) %all-to-all-start.2) | async-done | bytes 180256 | tf_op jit(solution)/shard_map/all_to_all | solution.py:139
  (100 shorter events, 29.5 us)
Async XLA Ops:
  0.6 9.2 %copy-start.3 = (bf16[1,20,64,128]{3,2,1,0:T(8,128)(2,1)S(1)}, bf16[1,20,64,128]{3,2,1,0:T(8,128)(2,1)}, u32[]{:S(2)}) copy-start(bf16[1,20,64,128]{3,2,1,0:T(8,128)(2,1)} %param.7) | copy-start | bytes 983044
  1.4 6.5 %collective-permute-start = (bf16[1,64,128]{2,1,0:T(8,128)(2,1)S(1)}, bf16[1,64,128]{2,1,0:T(8,128)(2,1)S(1)}, u32[]{:S(2)}, u32[]{:S(2)}) collective-permute-start(bf16[1,64,128]{2,1,0:T(8,128)(2,1)S(1)} %get-tuple-element.42), channel_id=1, source_target_pairs={{0,16},{16,32},{32,48},{48,64},{64,80},{80,96},{96,112},{1,17},{17... | collective-permute-start | bytes 49160 | tf_op jit(solution)/shard_map/ppermute | solution.py:18
  5.4 4.5 %collective-permute-start.1 = (bf16[1,64,128]{2,1,0:T(8,128)(2,1)S(1)}, bf16[1,64,128]{2,1,0:T(8,128)(2,1)S(1)}, u32[]{:S(2)}, u32[]{:S(2)}) collective-permute-start(bf16[1,64,128]{2,1,0:T(8,128)(2,1)S(1)} %get-tuple-element.43), channel_id=1, source_target_pairs={{16,0},{32,16},{48,32},{64,48},{80,64},{96,80},{112,96},{17,1},{33... | collective-permute-start | bytes 49160 | tf_op jit(solution)/shard_map/ppermute | solution.py:21
  10.1 10.6 %collective-permute-start.2 = (bf16[22,64,1]{2,1,0:T(8,128)(2,1)S(1)}, bf16[22,64,1]{2,1,0:T(8,128)(2,1)S(1)}, u32[]{:S(2)}, u32[]{:S(2)}) collective-permute-start(bf16[22,64,1]{2,1,0:T(8,128)(2,1)S(1)} %get-tuple-element.38), channel_id=1, source_target_pairs={{0,1},{1,2},{2,3},{3,4},{4,5},{5,6},{6,7},{7,8},{8,9},{9,10},{10,1... | collective-permute-start | bytes 8456 | tf_op jit(solution)/shard_map/ppermute | solution.py:18
  15.0 21.1 %collective-permute-start.3 = (bf16[22,64,1]{2,1,0:T(8,128)(2,1)S(1)}, bf16[22,64,1]{2,1,0:T(8,128)(2,1)S(1)}, u32[]{:S(2)}, u32[]{:S(2)}) collective-permute-start(bf16[22,64,1]{2,1,0:T(8,128)(2,1)S(1)} %get-tuple-element.39), channel_id=1, source_target_pairs={{1,0},{2,1},{3,2},{4,3},{5,4},{6,5},{7,6},{8,7},{9,8},{10,9},{11,1... | collective-permute-start | bytes 8456 | tf_op jit(solution)/shard_map/ppermute | solution.py:21
  39.5 31.0 %collective-permute-start.6 = (bf16[20,64,128]{2,1,0:T(8,128)(2,1)S(1)}, bf16[20,64,128]{2,1,0:T(8,128)(2,1)S(1)}, u32[]{:S(2)}, u32[]{:S(2)}) collective-permute-start(bf16[20,64,128]{2,1,0:T(8,128)(2,1)S(1)} %get-tuple-element.48.feat_ref), channel_id=1, source_target_pairs={{0,4},{1,5},{2,6},{3,7},{4,8},{5,9},{6,10},{7,11},{8,12},{9,13},{1... | collective-permute-start | bytes 983048 | tf_op jit(solution)/shard_map/ppermute | solution.py:117
  39.5 31.0 %collective-permute-start.5 = (bf16[20,64,128]{2,1,0:T(8,128)(2,1)S(1)}, bf16[20,64,128]{2,1,0:T(8,128)(2,1)S(1)}, u32[]{:S(2)}, u32[]{:S(2)}) collective-permute-start(bf16[20,64,128]{2,1,0:T(8,128)(2,1)S(1)} %get-tuple-element.48.feat_ref), channel_id=1, source_target_pairs={{0,8},{1,9},{2,10},{3,11},{4,12},{5,13},{6,14},{7,15},{8,0},{9,1},... | collective-permute-start | bytes 983048 | tf_op jit(solution)/shard_map/ppermute | solution.py:117
  39.5 31.0 %collective-permute-start.4 = (bf16[20,64,128]{2,1,0:T(8,128)(2,1)S(1)}, bf16[20,64,128]{2,1,0:T(8,128)(2,1)S(1)}, u32[]{:S(2)}, u32[]{:S(2)}) collective-permute-start(bf16[20,64,128]{2,1,0:T(8,128)(2,1)S(1)} %get-tuple-element.48.feat_ref), channel_id=1, source_target_pairs={{0,12},{1,13},{2,14},{3,15},{4,0},{5,1},{6,2},{7,3},{8,4},{9,5},{1... | collective-permute-start | bytes 983048 | tf_op jit(solution)/shard_map/ppermute | solution.py:117
  70.5 34.1 %copy-start = (bf16[1,20,64,128]{3,2,1,0:T(8,128)(2,1)S(1)}, bf16[1,20,64,128]{3,2,1,0:T(8,128)(2,1)}, u32[]{:S(2)}) copy-start(bf16[1,20,64,128]{3,2,1,0:T(8,128)(2,1)} %param.8) | copy-start | bytes 983044
  70.5 34.1 %copy-start.1 = (bf16[64,64]{1,0:T(8,128)(2,1)S(1)}, bf16[64,64]{1,0:T(8,128)(2,1)}, u32[]{:S(2)}) copy-start(bf16[64,64]{1,0:T(8,128)(2,1)} %wq_ref.1) | copy-start | bytes 24580
  70.5 34.1 %copy-start.2 = (bf16[64,64]{1,0:T(8,128)(2,1)S(1)}, bf16[64,64]{1,0:T(8,128)(2,1)}, u32[]{:S(2)}) copy-start(bf16[64,64]{1,0:T(8,128)(2,1)} %wk_ref.1) | copy-start | bytes 24580
  71.5 33.1 %collective-permute-start.10 = (bf16[20,64,128]{2,1,0:T(8,128)(2,1)}, bf16[20,64,128]{2,1,0:T(8,128)(2,1)S(1)}, u32[]{:S(2)}, u32[]{:S(2)}) collective-permute-start(bf16[20,64,128]{2,1,0:T(8,128)(2,1)} %get-tuple-element.26), channel_id=1, source_target_pairs={{0,131},{1,128},{2,129},{3,130},{4,135},{5,132},{6,133},{7,134},{8... | collective-permute-start | bytes 983048 | tf_op jit(solution)/shard_map/ppermute | solution.py:127
  75.8 28.8 %collective-permute-start.9 = (bf16[20,64,128]{2,1,0:T(8,128)(2,1)S(1)}, bf16[20,64,128]{2,1,0:T(8,128)(2,1)S(1)}, u32[]{:S(2)}, u32[]{:S(2)}) collective-permute-start(bf16[20,64,128]{2,1,0:T(8,128)(2,1)S(1)} %get-tuple-element.27), channel_id=1, source_target_pairs={{0,130},{1,131},{2,128},{3,129},{4,134},{5,135},{6,132},{7,133},{8... | collective-permute-start | bytes 983048 | tf_op jit(solution)/shard_map/ppermute | solution.py:127
  77.2 27.4 %collective-permute-start.8 = (bf16[20,64,128]{2,1,0:T(8,128)(2,1)S(1)}, bf16[20,64,128]{2,1,0:T(8,128)(2,1)S(1)}, u32[]{:S(2)}, u32[]{:S(2)}) collective-permute-start(bf16[20,64,128]{2,1,0:T(8,128)(2,1)S(1)} %get-tuple-element.28), channel_id=1, source_target_pairs={{0,129},{1,130},{2,131},{3,128},{4,133},{5,134},{6,135},{7,132},{8... | collective-permute-start | bytes 983048 | tf_op jit(solution)/shard_map/ppermute | solution.py:127
  78.1 26.5 %collective-permute-start.7 = (bf16[20,64,128]{2,1,0:T(8,128)(2,1)S(1)}, bf16[20,64,128]{2,1,0:T(8,128)(2,1)S(1)}, u32[]{:S(2)}, u32[]{:S(2)}) collective-permute-start(bf16[20,64,128]{2,1,0:T(8,128)(2,1)S(1)} %get-tuple-element.29), channel_id=1, source_target_pairs={{0,128},{1,129},{2,130},{3,131},{4,132},{5,133},{6,134},{7,135},{8... | collective-permute-start | bytes 983048 | tf_op jit(solution)/shard_map/ppermute | solution.py:127
  122.6 7.0 %collective-permute-start.11 = (bf16[20,64,128]{2,1,0:T(8,128)(2,1)S(1)}, bf16[20,64,128]{2,1,0:T(8,128)(2,1)S(1)}, u32[]{:S(2)}, u32[]{:S(2)}) collective-permute-start(bf16[20,64,128]{2,1,0:T(8,128)(2,1)S(1)} %get-tuple-element.15), channel_id=1, source_target_pairs={{0,128},{1,129},{2,130},{3,131},{4,132},{5,133},{6,134},{7,135},{8... | collective-permute-start | bytes 983048 | tf_op jit(solution)/shard_map/ppermute | solution.py:127
  123.2 32.2 %collective-permute-start.12 = (bf16[20,64,128]{2,1,0:T(8,128)(2,1)S(1)}, bf16[20,64,128]{2,1,0:T(8,128)(2,1)S(1)}, u32[]{:S(2)}, u32[]{:S(2)}) collective-permute-start(bf16[20,64,128]{2,1,0:T(8,128)(2,1)S(1)} %get-tuple-element.16), channel_id=1, source_target_pairs={{0,131},{1,128},{2,129},{3,130},{4,135},{5,132},{6,133},{7,134},{8... | collective-permute-start | bytes 983048 | tf_op jit(solution)/shard_map/ppermute | solution.py:127
  127.2 28.2 %collective-permute-start.13 = (bf16[20,64,128]{2,1,0:T(8,128)(2,1)S(1)}, bf16[20,64,128]{2,1,0:T(8,128)(2,1)S(1)}, u32[]{:S(2)}, u32[]{:S(2)}) collective-permute-start(bf16[20,64,128]{2,1,0:T(8,128)(2,1)S(1)} %get-tuple-element.17), channel_id=1, source_target_pairs={{0,130},{1,131},{2,128},{3,129},{4,134},{5,135},{6,132},{7,133},{8... | collective-permute-start | bytes 983048 | tf_op jit(solution)/shard_map/ppermute | solution.py:127
  127.2 50.1 %copy-start.8 = (f32[20,64,128]{2,1,0:T(8,128)S(1)}, f32[20,64,128]{2,1,0:T(8,128)}, u32[]{:S(2)}) copy-start(f32[20,64,128]{2,1,0:T(8,128)} %get-tuple-element.49) | copy-start | bytes 1966084
  127.2 28.1 %collective-permute-start.14 = (bf16[20,64,128]{2,1,0:T(8,128)(2,1)S(1)}, bf16[20,64,128]{2,1,0:T(8,128)(2,1)S(1)}, u32[]{:S(2)}, u32[]{:S(2)}) collective-permute-start(bf16[20,64,128]{2,1,0:T(8,128)(2,1)S(1)} %get-tuple-element.18), channel_id=1, source_target_pairs={{0,129},{1,130},{2,131},{3,128},{4,133},{5,134},{6,135},{7,132},{8... | collective-permute-start | bytes 983048 | tf_op jit(solution)/shard_map/ppermute | solution.py:127
  156.9 9.9 %collective-permute-start.15 = (bf16[20,64,128]{2,1,0:T(8,128)(2,1)}, bf16[20,64,128]{2,1,0:T(8,128)(2,1)S(1)}, u32[]{:S(2)}, u32[]{:S(2)}) collective-permute-start(bf16[20,64,128]{2,1,0:T(8,128)(2,1)} %get-tuple-element.23), channel_id=1, source_target_pairs={{0,12},{1,13},{2,14},{3,15},{4,0},{5,1},{6,2},{7,3},{8,4},{9,5},{1... | collective-permute-start | bytes 983048 | tf_op jit(solution)/shard_map/ppermute | solution.py:117
  159.5 9.9 %collective-permute-start.16 = (bf16[20,64,128]{2,1,0:T(8,128)(2,1)}, bf16[20,64,128]{2,1,0:T(8,128)(2,1)}, u32[]{:S(2)}, u32[]{:S(2)}) collective-permute-start(bf16[20,64,128]{2,1,0:T(8,128)(2,1)} %get-tuple-element.24), channel_id=1, source_target_pairs={{0,8},{1,9},{2,10},{3,11},{4,12},{5,13},{6,14},{7,15},{8,0},{9,1},... | collective-permute-start | bytes 983048 | tf_op jit(solution)/shard_map/ppermute | solution.py:117
  159.5 17.8 %collective-permute-start.17 = (bf16[20,64,128]{2,1,0:T(8,128)(2,1)}, bf16[20,64,128]{2,1,0:T(8,128)(2,1)}, u32[]{:S(2)}, u32[]{:S(2)}) collective-permute-start(bf16[20,64,128]{2,1,0:T(8,128)(2,1)} %get-tuple-element.25), channel_id=1, source_target_pairs={{0,4},{1,5},{2,6},{3,7},{4,8},{5,9},{6,10},{7,11},{8,12},{9,13},{1... | collective-permute-start | bytes 983048 | tf_op jit(solution)/shard_map/ppermute | solution.py:117
  166.8 10.6 %copy-start.10 = (bf16[20,64,128]{2,1,0:T(8,128)(2,1)}, bf16[20,64,128]{2,1,0:T(8,128)(2,1)S(1)}, u32[]{:S(2)}) copy-start(bf16[20,64,128]{2,1,0:T(8,128)(2,1)S(1)} %collective-permute-done.15) | copy-start | bytes 983044
  180.2 8.0 %collective-permute-start.18 = (bf16[1,64,128]{2,1,0:T(8,128)(2,1)S(1)}, bf16[1,64,128]{2,1,0:T(8,128)(2,1)S(1)}, u32[]{:S(2)}, u32[]{:S(2)}) collective-permute-start(bf16[1,64,128]{2,1,0:T(8,128)(2,1)S(1)} %get-tuple-element.40), channel_id=1, source_target_pairs={{0,16},{16,32},{32,48},{48,64},{64,80},{80,96},{96,112},{1,17},{17... | collective-permute-start | bytes 49160 | tf_op jit(solution)/shard_map/ppermute | solution.py:18
  184.0 4.5 %collective-permute-start.19 = (bf16[1,64,128]{2,1,0:T(8,128)(2,1)S(1)}, bf16[1,64,128]{2,1,0:T(8,128)(2,1)S(1)}, u32[]{:S(2)}, u32[]{:S(2)}) collective-permute-start(bf16[1,64,128]{2,1,0:T(8,128)(2,1)S(1)} %get-tuple-element.41), channel_id=1, source_target_pairs={{16,0},{32,16},{48,32},{64,48},{80,64},{96,80},{112,96},{17,1},{33... | collective-permute-start | bytes 49160 | tf_op jit(solution)/shard_map/ppermute | solution.py:21
  187.5 15.3 %collective-permute-start.22 = (f32[704,64]{1,0:T(8,128)S(1)}, f32[704,64]{1,0:T(8,128)S(1)}, u32[]{:S(2)}, u32[]{:S(2)}) collective-permute-start(f32[704,64]{1,0:T(8,128)S(1)} %constant_dynamic-update-slice_fusion), channel_id=1, source_target_pairs={{0,128},{128,0},{1,129},{129,1},{2,130},{130,2},{3,131},{131,3},{4... | collective-permute-start | bytes 540680 | tf_op jit(solution)/shard_map/ppermute | solution.py:131
  188.8 12.7 %collective-permute-start.20 = (bf16[22,64,1]{2,1,0:T(8,128)(2,1)S(1)}, bf16[22,64,1]{2,1,0:T(8,128)(2,1)S(1)}, u32[]{:S(2)}, u32[]{:S(2)}) collective-permute-start(bf16[22,64,1]{2,1,0:T(8,128)(2,1)S(1)} %get-tuple-element.34), channel_id=1, source_target_pairs={{1,0},{2,1},{3,2},{4,3},{5,4},{6,5},{7,6},{8,7},{9,8},{10,9},{11,1... | collective-permute-start | bytes 8456 | tf_op jit(solution)/shard_map/ppermute | solution.py:21
  190.1 12.2 %collective-permute-start.21 = (bf16[22,64,1]{2,1,0:T(8,128)(2,1)S(1)}, bf16[22,64,1]{2,1,0:T(8,128)(2,1)S(1)}, u32[]{:S(2)}, u32[]{:S(2)}) collective-permute-start(bf16[22,64,1]{2,1,0:T(8,128)(2,1)S(1)} %get-tuple-element.35), channel_id=1, source_target_pairs={{0,1},{1,2},{2,3},{3,4},{4,5},{5,6},{6,7},{7,8},{8,9},{9,10},{10,1... | collective-permute-start | bytes 8456 | tf_op jit(solution)/shard_map/ppermute | solution.py:18
  205.4 23.5 %all-to-all-start = ((f32[8,88,64]{1,2,0:T(8,128)}), f32[8,88,64]{1,2,0:T(8,128)S(1)}, u32[]{:S(2)}, u32[]{:S(2)}) async-start(f32[8,88,64]{1,2,0:T(8,128)} %copy.94), calls=%async_computation | async-start | bytes 524288 | tf_op jit(solution)/shard_map/all_to_all | solution.py:135
  229.8 21.9 %all-to-all-start.1 = ((f32[16,88,64]{1,2,0:T(8,128)}), f32[16,88,64]{1,2,0:T(8,128)}, u32[]{:S(2)}, u32[]{:S(2)}) async-start(f32[16,88,64]{1,2,0:T(8,128)} %broadcast_in_dim.44), calls=%async_computation.1 | async-start | bytes 1048576 | tf_op jit(solution)/shard_map/all_to_all | solution.py:137
  253.6 9.4 %all-to-all-start.2 = ((f32[8,88,64]{1,2,0:T(8,128)}), f32[8,88,64]{1,2,0:T(8,128)S(1)}, u32[]{:S(2)}, u32[]{:S(2)}) async-start(f32[8,88,64]{1,2,0:T(8,128)} %broadcast_in_dim.45), calls=%async_computation.2 | async-start | bytes 524288 | tf_op jit(solution)/shard_map/all_to_all | solution.py:139
  (6 other events, 22.1 us)
